TPU v7x, 32 devices: a whole 2x2x4 slice. The times are simulated.
32 devices in a mesh: dp: 4 (over y, x), seq: 8 (over z, core).
Axes of the slice: x: 2, y: 2, z: 4, core: 2. Of those that a mesh axis runs over, the one named last changes fastest.
Arguments:
- byte_ids: int32 [4, 4096], P('dp', 'seq'), may hold values from 0 to 255
- embedding: bfloat16 [256, 1024], replicated, may hold values from -6 to 6
- cotangent: bfloat16 [4, 4096, 1024], P('dp', 'seq'), may hold values from -6 to 6
- norm_gain: float32 [1024], replicated, may hold values from 0.5 to 1.5
- input_projection_weight: bfloat16 [1024, 4096], replicated, may hold values from -0.1875 to 0.1875
- conv_weight: float32 [4, 2048], replicated, may hold values from -3 to 3
- conv_bias: float32 [2048], replicated, may hold values from -3 to 3
- select_weight: bfloat16 [2048, 96], replicated, may hold values from -0.125 to 0.125
- step_weight: bfloat16 [64, 2048], replicated, may hold values from -0.75 to 0.75
- step_bias: float32 [2048], replicated, may hold values from -7 to -3
- decay_log: float32 [16, 2048], replicated, may hold values from -5 to 1
- skip_gain: float32 [2048], replicated, may hold values from 0.5 to 1.5
- output_projection_weight: bfloat16 [2048, 1024], replicated, may hold values from -0.5 to 0.5
Outputs:
- output: bfloat16 [4, 4096, 1024], P('dp', 'seq')
- d_inputs: float32 [4, 4096, 1024], P('dp', 'seq')
- d_embedding: float32 [256, 1024], replicated
- d_norm_gain: float32 [1024], replicated
- d_input_weight: float32 [1024, 4096], replicated
- d_conv_weight: float32 [4, 2048], replicated
- d_conv_bias: float32 [2048], replicated
- d_select_weight: float32 [2048, 96], replicated
- d_step_weight: float32 [64, 2048], replicated
- d_step_bias: float32 [2048], replicated
- d_decay_log: float32 [16, 2048], replicated
- d_skip_gain: float32 [2048], replicated
- d_output_weight: float32 [2048, 1024], replicated
All inputs are finite; a program needn't handle non-finite values.
Results may differ from a plain program's by a relative error of at most 0.0087.
The roundings to bfloat16 on the way count: a program that leaves them out, or rounds other values in their place, can miss the bound.
Values may be sent and summed in bfloat16 or wider, within the bound.
A program may use at most 192 MiB of HBM per device.

v0:
```python
import jax
import jax.numpy as jnp
from jax import lax
from jax.sharding import PartitionSpec as P

BLOCK = 16


EPS = 1e-05


def passed_along(value, axis, by):
    peers = lax.axis_size(axis)
    pairs = [(i, i + by) for i in range(peers) if 0 <= i + by < peers]
    return lax.ppermute(value, axis, pairs)


def prefix(part, axis, combine, identity, reverse):
    count = lax.axis_size(axis)
    place = lax.axis_index(axis)
    ahead = count - 1 - place if reverse else place
    gathered = jax.tree.map(lambda a: lax.all_gather(a, axis), part)
    state = jax.tree.map(lambda a, e: jnp.zeros_like(a) + jnp.asarray(e, a.dtype), part, identity)

    def one(turn, state):
        source = count - 1 - turn if reverse else turn
        return combine(
            state, jax.tree.map(lambda a: lax.dynamic_index_in_dim(a, source, 0, False), gathered)
        )

    return lax.fori_loop(0, ahead, one, state)


def silu_slope(value):
    sigma = jax.nn.sigmoid(value)
    return sigma * (1.0 + value * (1.0 - sigma))


def chain_link(earlier, later):
    return (earlier[0] * later[0], later[0] * earlier[1] + later[1])


def contract_rows(left, right):
    return lax.dot_general(
        left, right, (((0,), (0,)), ((), ())), preferred_element_type=jnp.float32
    )


def contract_cols(left, right):
    return lax.dot_general(
        left, right, (((1,), (1,)), ((), ())), preferred_element_type=jnp.float32
    )


def cut_block(arrays, index, depth):
    return tuple((lax.dynamic_slice_in_dim(array, index * depth, depth, 1) for array in arrays))


def grow_block(state, delta_block, active_block, inject_block, rates):
    kept = []
    factors = []
    for place in range(delta_block.shape[1]):
        factor = jnp.exp(delta_block[:, place, None, :] * rates)
        drive = (delta_block[:, place] * active_block[:, place])[:, None, :] * inject_block[
            :, place, :, None
        ]
        state = factor * state + drive
        kept.append(state)
        factors.append(factor)
    return (kept, factors)


def unblock(array):
    moved = jnp.swapaxes(array, 0, 1)
    return moved.reshape(moved.shape[0] * moved.shape[1] * moved.shape[2], moved.shape[3])


def on_device(
    byte_ids,
    embedding,
    cotangent,
    norm_gain,
    input_projection_weight,
    conv_weight,
    conv_bias,
    select_weight,
    step_weight,
    step_bias,
    decay_log,
    skip_gain,
    output_projection_weight,
):
    count, stretch = byte_ids.shape
    vocab, width = embedding.shape
    kernel, inner = conv_weight.shape
    states = decay_log.shape[0]
    rank = step_weight.shape[0]
    rows = count * stretch
    depth = BLOCK
    blocks = stretch // depth
    one_hot = byte_ids.reshape(rows, 1) == jnp.arange(vocab, dtype=jnp.int32)[None, :]
    block_inputs = jnp.dot(
        one_hot.astype(jnp.bfloat16), embedding, preferred_element_type=jnp.float32
    )
    scale = lax.rsqrt(jnp.mean(block_inputs * block_inputs, axis=1, keepdims=True) + EPS)
    normed_input = (block_inputs * scale * norm_gain).astype(jnp.bfloat16)
    inner_and_gate = jnp.dot(
        normed_input, input_projection_weight, preferred_element_type=jnp.float32
    ).astype(jnp.bfloat16)
    front = inner_and_gate[:, :inner].reshape(count, stretch, inner)
    gate = inner_and_gate[:, inner:].astype(jnp.float32)
    tail = passed_along(front[:, stretch - (kernel - 1) :, :], "seq", 1)
    extended = jnp.concatenate([tail, front], axis=1).astype(jnp.float32)
    mixed = conv_bias + conv_weight[0] * extended[:, 0:stretch]
    for place in range(1, kernel):
        mixed = mixed + conv_weight[place] * extended[:, place : place + stretch]
    active = jax.nn.silu(mixed).astype(jnp.bfloat16)
    active_flat = active.reshape(rows, inner)
    active_real = active.astype(jnp.float32)
    select = jnp.dot(active_flat, select_weight, preferred_element_type=jnp.float32).astype(
        jnp.bfloat16
    )
    lowrank = select[:, :rank]
    inject = select[:, rank : rank + states].astype(jnp.float32).reshape(count, stretch, states)
    readout = select[:, rank + states :].astype(jnp.float32).reshape(count, stretch, states)
    pre = jnp.dot(lowrank, step_weight, preferred_element_type=jnp.float32) + step_bias
    delta = jax.nn.softplus(pre).reshape(count, stretch, inner)
    rates = -jnp.exp(decay_log)
    zero_state = jnp.zeros((count, states, inner), jnp.float32)

    def local_pass(state, index):
        delta_block, active_block, inject_block = cut_block(
            (delta, active_real, inject), index, depth
        )
        kept, factors = grow_block(state, delta_block, active_block, inject_block, rates)
        return (kept[-1], None)

    local_end, unused = lax.scan(local_pass, zero_state, jnp.arange(blocks))
    decay_total = jnp.exp(jnp.sum(delta, axis=1)[:, None, :] * rates)
    identity = (jnp.ones_like(decay_total), jnp.zeros_like(local_end))
    start_state = prefix((decay_total, local_end), "seq", chain_link, identity, False)[1]

    def full_pass(state, index):
        delta_block, active_block, inject_block, readout_block = cut_block(
            (delta, active_real, inject, readout), index, depth
        )
        kept, factors = grow_block(state, delta_block, active_block, inject_block, rates)
        values = jnp.stack(
            [
                jnp.sum(readout_block[:, place, :, None] * kept[place], axis=1)
                for place in range(depth)
            ],
            axis=1,
        )
        return (kept[-1], (state, values))

    unused, (block_starts, block_out) = lax.scan(full_pass, start_state, jnp.arange(blocks))
    scanned = unblock(block_out) + skip_gain * active_real.reshape(rows, inner)
    gate_value = jax.nn.silu(gate)
    gated_output = (scanned * gate_value).astype(jnp.bfloat16)
    result = block_inputs + jnp.dot(
        gated_output, output_projection_weight, preferred_element_type=jnp.float32
    )
    output = result.astype(jnp.bfloat16).reshape(count, stretch, width)
    upstream = cotangent.reshape(rows, width)
    d_output_weight = contract_rows(gated_output, upstream)
    d_gated = contract_cols(upstream, output_projection_weight)
    d_scanned = d_gated * gate_value
    d_gate = d_gated * scanned * silu_slope(gate)
    d_skip_gain = jnp.sum(d_scanned * active_real.reshape(rows, inner), axis=0)
    grad_scan = d_scanned.reshape(count, stretch, inner)

    def back_local(carry, index):
        delta_block, readout_block, grad_block = cut_block(
            (delta, readout, grad_scan), index, depth
        )
        for place in range(depth - 1, -1, -1):
            adjoint = readout_block[:, place, :, None] * grad_block[:, place, None, :] + carry
            carry = jnp.exp(delta_block[:, place, None, :] * rates) * adjoint
        return (carry, None)

    local_message, unused = lax.scan(back_local, zero_state, jnp.arange(blocks), reverse=True)
    incoming = prefix((decay_total, local_message), "seq", chain_link, identity, True)[1]

    def back_full(carry, packed):
        index, begin = packed
        delta_block, active_block, inject_block, readout_block, grad_block = cut_block(
            (delta, active_real, inject, readout, grad_scan), index, depth
        )
        kept, factors = grow_block(begin, delta_block, active_block, inject_block, rates)
        adjoint_carry, rate_total = carry
        pieces_read = []
        pieces_inject = []
        pieces_delta = []
        pieces_active = []
        for place in range(depth - 1, -1, -1):
            before = begin if place == 0 else kept[place - 1]
            delta_now = delta_block[:, place]
            active_now = active_block[:, place]
            grad_now = grad_block[:, place]
            adjoint = readout_block[:, place, :, None] * grad_now[:, None, :] + adjoint_carry
            through = adjoint * before * factors[place]
            weighted = jnp.sum(adjoint * inject_block[:, place, :, None], axis=1)
            pieces_read.append(jnp.sum(grad_now[:, None, :] * kept[place], axis=2))
            pieces_inject.append(jnp.sum(adjoint * (delta_now * active_now)[:, None, :], axis=2))
            pieces_delta.append(jnp.sum(through * rates, axis=1) + active_now * weighted)
            pieces_active.append(delta_now * weighted)
            rate_total = rate_total + jnp.sum(through * delta_now[:, None, :], axis=0)
            adjoint_carry = factors[place] * adjoint
        stacked = tuple(
            (
                jnp.stack(pieces[::-1], axis=1)
                for pieces in (pieces_read, pieces_inject, pieces_delta, pieces_active)
            )
        )
        return ((adjoint_carry, rate_total), stacked)

    carry_out, block_grads = lax.scan(
        back_full,
        (incoming, jnp.zeros((states, inner), jnp.float32)),
        (jnp.arange(blocks), block_starts),
        reverse=True,
    )
    d_readout = unblock(block_grads[0])
    d_inject = unblock(block_grads[1])
    d_delta = unblock(block_grads[2])
    d_active_scan = unblock(block_grads[3])
    d_decay_log = carry_out[1] * rates
    d_pre = d_delta * jax.nn.sigmoid(pre)
    d_step_bias = jnp.sum(d_pre, axis=0)
    d_pre_low = d_pre.astype(jnp.bfloat16)
    d_step_weight = contract_rows(lowrank, d_pre_low)
    d_lowrank = contract_cols(d_pre_low, step_weight)
    d_select = jnp.concatenate([d_lowrank, d_inject, d_readout], axis=1).astype(jnp.bfloat16)
    d_select_weight = contract_rows(active_flat, d_select)
    d_active = skip_gain * d_scanned + d_active_scan + contract_cols(d_select, select_weight)
    d_mixed = d_active.reshape(count, stretch, inner) * silu_slope(mixed)
    d_conv_bias = jnp.sum(d_mixed, axis=(0, 1))
    d_conv_weight = jnp.stack(
        [
            jnp.sum(d_mixed * extended[:, place : place + stretch], axis=(0, 1))
            for place in range(kernel)
        ]
    )
    after = passed_along(d_mixed[:, : kernel - 1], "seq", -1)
    spread = jnp.concatenate([d_mixed, after], axis=1)
    d_front = conv_weight[kernel - 1] * spread[:, 0:stretch]
    for place in range(1, kernel):
        d_front = d_front + conv_weight[kernel - 1 - place] * spread[:, place : place + stretch]
    d_both = jnp.concatenate([d_front.reshape(rows, inner), d_gate], axis=1).astype(jnp.bfloat16)
    d_input_weight = contract_rows(normed_input, d_both)
    d_normed = contract_cols(d_both, input_projection_weight)
    d_norm_gain = jnp.sum(d_normed * block_inputs * scale, axis=0)
    scaled = norm_gain * d_normed
    cubed = scale * scale * scale
    d_inputs = (
        upstream.astype(jnp.float32)
        + scale * scaled
        - block_inputs * cubed * jnp.mean(scaled * block_inputs, axis=1, keepdims=True)
    )
    d_embedding = lax.dot_general(
        one_hot.astype(jnp.float32),
        d_inputs,
        (((0,), (0,)), ((), ())),
        precision=lax.Precision.HIGHEST,
        preferred_element_type=jnp.float32,
    )
    large = (d_input_weight.reshape(-1), d_output_weight.reshape(-1), d_embedding.reshape(-1))
    shares = (
        lax.psum_scatter(large[0], ("dp", "seq"), scatter_dimension=0, tiled=True),
        lax.psum_scatter(large[1], ("dp", "seq"), scatter_dimension=0, tiled=True),
        lax.psum_scatter(large[2], ("dp", "seq"), scatter_dimension=0, tiled=True),
    )
    whole = (
        lax.all_gather(shares[0], ("dp", "seq"), axis=0, tiled=True),
        lax.all_gather(shares[1], ("dp", "seq"), axis=0, tiled=True),
        lax.all_gather(shares[2], ("dp", "seq"), axis=0, tiled=True),
    )
    small = lax.psum(
        (
            d_norm_gain,
            d_conv_weight,
            d_conv_bias,
            d_select_weight,
            d_step_weight,
            d_step_bias,
            d_decay_log,
            d_skip_gain,
        ),
        ("dp", "seq"),
    )
    return (
        output,
        d_inputs.reshape(count, stretch, width),
        whole[2].reshape(vocab, width),
        small[0],
        whole[0].reshape(width, 2 * inner),
        small[1],
        small[2],
        small[3],
        small[4],
        small[5],
        small[6],
        small[7],
        whole[1].reshape(inner, width),
    )


def solution(mesh):
    placed = (
        P("dp", "seq"),
        P(),
        P("dp", "seq", None),
        P(),
        P(),
        P(),
        P(),
        P(),
        P(),
        P(),
        P(),
        P(),
        P(),
    )
    return jax.shard_map(
        on_device,
        mesh=mesh,
        in_specs=placed,
        out_specs=(
            P("dp", "seq", None),
            P("dp", "seq", None),
            P(),
            P(),
            P(),
            P(),
            P(),
            P(),
            P(),
            P(),
            P(),
            P(),
            P(),
        ),
        check_vma=False,
    )
```

profile of v0, /device:TPU:0, one launch (start us, length us, event | category | flops | bytes accessed | tf_op | source)
XLA Modules:
  0.0 2893.0 jit_solution(1082002430508251063)
XLA Ops:
  10.8 8.5 convolution_convert_fusion
  19.5 2.6 collective-permute-start
  22.2 4.4 fusion.358
  27.4 3.0 copy-done.7
  30.3 7.9 fusion.343
  40.7 4.4 fusion.350
  46.0 175.3 %while.95 = (s32[]{:T(128)}, f32[1,16,2048]{2,1,0:T(8,128)S(1)}, s32[32]{0:T(128)S(1)}, f32[1,512,2048]{2,1,0:T(8,128)}, f32[16,2048]{1,0:T(8,128)S(1)}, /*index...) while((s32[]{:T(128)}, f32[1,16,2048]{2,1,0:T(8,128)S(1)}, ...), condition=%wide.region_25.26_spmd.clone, body=%wide.region_24.25_spmd.clone.sunk | while | flops 2129943 | bytes 1183353 | solution.py:182
  112.6 2.8 constant_dynamic-slice_fusion.290
  134.4 2.7 constant_dynamic-slice_fusion.290
  140.1 2.7 constant_dynamic-slice_fusion.290
  145.8 2.7 constant_dynamic-slice_fusion.290
  151.5 2.7 constant_dynamic-slice_fusion.290
  173.3 2.7 constant_dynamic-slice_fusion.290
  178.9 2.8 constant_dynamic-slice_fusion.290
  184.6 3.0 constant_dynamic-slice_fusion.290
  196.0 2.7 constant_dynamic-slice_fusion.290
  201.6 2.7 constant_dynamic-slice_fusion.290
  212.5 2.8 constant_dynamic-slice_fusion.290
  224.7 165.8 %while.94 = (s32[]{:T(128)}, f32[1,16,2048]{2,1,0:T(8,128)S(1)}, s32[32]{0:T(128)S(1)}, f32[1,512,2048]{2,1,0:T(8,128)}, f32[16,2048]{1,0:T(8,128)S(1)}, /*index...) while((s32[]{:T(128)}, f32[1,16,2048]{2,1,0:T(8,128)S(1)}, ...), condition=%wide.region_3.4_spmd.clone, body=%wide.region_2.3_spmd.clone.sunk | while | flops 2162710 | bytes 1183333 | solution.py:138
  391.4 7.4 while.93
  398.8 17.3 all-gather.18.cloned.1.call-done
  421.2 258.4 %while.92 = (s32[]{:T(128)}, f32[1,16,2048]{2,1,0:T(8,128)S(1)}, f32[32,1,16,2048]{3,2,1,0:T(8,128)}, f32[32,1,16,2048]{3,2,1,0:T(8,128)}, s32[32]{0:T(128)S(1)}...) while((s32[]{:T(128)}, f32[1,16,2048]{2,1,0:T(8,128)S(1)}, ...), condition=%wide.region_23.24_spmd, body=%wide.region_6.23_spmd.sunk | while | flops 4718613 | bytes 4005303 | solution.py:157
  686.5 1416.0 %while.96 = (s32[]{:T(128)}, f32[1,16,2048]{2,1,0:T(8,128)S(1)}, f32[16,2048]{1,0:T(8,128)S(1)}, bf16[32,1,16,16]{3,2,1,0:T(8,128)(2,1)}, bf16[32,1,16,16]{3,2,1...) while((s32[]{:T(128)}, f32[1,16,2048]{2,1,0:T(8,128)S(1)}, ...), condition=%wide.region_93.94_spmd.clone, body=%wide.region_28.93_spmd.clone.sunk | while | flops 26115608 | bytes 15927061 | solution.py:218
  761.2 2.6 stack.469
  805.1 2.6 stack.469
  849.2 2.6 stack.469
  893.2 2.6 stack.469
  937.8 2.6 stack.469
  1070.6 2.6 stack.469
  1114.8 2.6 stack.469
  1159.2 2.6 stack.469
  2102.5 6.0 fusion.382
  2111.1 6.6 fusion.339
  2121.0 3.2 bitcast_multiply_fusion.85
  2126.2 4.4 convolution_bitcast_fusion.1
  2132.0 5.5 copy.66
  2137.5 8.7 multiply_reduce_fusion.67
  2146.3 9.4 multiply_reduce_fusion.68
  2155.7 4.7 convolution_bitcast_fusion
  2166.4 7.0 copy.65
  2173.6 436.9 %all-reduce.7.cloned.1.call-done = (f32[262144]{0:T(1024)}, f32[4194304]{0:T(1024)}, f32[2048,96]{0,1:T(8,128)}, f32[64,2048]{1,0:T(8,128)}, f32[16,2048]{1,0:T(8,128)}, /*index=5*/f32[2097152]{0:T(1024)}) async-done(((f32[262144]{0:T(1024)}, f32[4194304]{0:T(1024)}, f32[2048,96]{0,1:T(8,128)}, f32[64,2048]{1,0:T(8,128)}, f32[16,2048]{1,0:T(8,128)}, /*index=5*/f32[2097152]{0:T(1024)}), (f32[262144]{0:T(1024)}, ...) | async-done | bytes 27656208
  2615.8 6.1 fusion.353
  2622.0 40.4 %all-reduce.3 = (f32[1024]{0:T(1024)}, f32[4,2048]{1,0:T(4,128)}, f32[2048]{0:T(1024)}, f32[2048]{0:T(1024)}, f32[2048]{0:T(1024)}) all-reduce(f32[1024]{0:T(1024)S(1)} %get-tuple-element.1007, f32[4,2048]{1,0:T(4,128)S(1)} %pad_maximum_fusion.7, f32[2048]{0:T(1024)S(1)} %get-tuple-element.1006, ...), channel_id=1, replica_groups=mesh['dp'=4,'seq'=8] {'dp','seq'}, use_global_device_ids=true, to_apply=%region_97.98 | all-reduce | flops 15360 | bytes 122880 | tf_op jit(solution)/shard_map/psum | solution.py:279
  2662.4 4.9 all-gather.10.cloned.1.call-done
  2669.6 77.9 %all-gather.14.cloned.1.call-done = f32[2097152]{0:T(1024)} async-done(((f32[65536]{0:T(1024)}), f32[2097152]{0:T(1024)}) %all-gather.14.cloned.1.call-update) | async-done | bytes 8388624 | tf_op jit(solution)/shard_map/all_gather | solution.py:276
  2747.5 9.2 reshape.25110
  2756.8 108.3 %all-gather.12.cloned.1.call-done = f32[4194304]{0:T(1024)} async-done(((f32[131072]{0:T(1024)}), f32[4194304]{0:T(1024)}) %all-gather.12.cloned.1.call-update) | async-done | bytes 16777232 | tf_op jit(solution)/shard_map/all_gather | solution.py:275
  2865.1 18.2 reshape.25108
  (3199 shorter events, 1922.0 us)
Async XLA Ops:
  7.2 384.2 %all-gather.16.cloned.1.call-start = ((), (), s32[]{:S(2)}) async-start(), calls=%async_computation.3 | async-start | bytes 1179648 | tf_op jit(solution)/shard_map/all_gather | solution.py:22
  19.5 7.2 collective-permute-start
  45.7 345.6 %all-gather.20.cloned.1.call-start = ((), (), s32[]{:S(2)}) async-start(), calls=%async_computation.5 | async-start | bytes 1179648 | tf_op jit(solution)/shard_map/all_gather | solution.py:22
  224.7 191.4 %all-gather.18.cloned.1.call-start = ((), (), s32[]{:S(2)}) async-start(), calls=%async_computation.4 | async-start | bytes 1179648 | tf_op jit(solution)/shard_map/all_gather | solution.py:22
  391.3 2219.2 %all-reduce.7.cloned.1.call-start = ((), (), s32[]{:S(2)}) async-start(), calls=%async_computation.6 | async-start | bytes 55312384
  910.3 25.4 copy-start.18
  910.3 25.4 copy-start.19
  910.4 25.4 copy-start.23
  910.4 25.4 copy-start.24
  910.4 25.4 copy-start.25
  910.4 25.4 copy-start.31
  910.4 25.4 copy-start.32
  910.4 25.4 copy-start.36
  910.4 25.4 copy-start.37
  910.4 25.4 copy-start.42
  1397.8 25.1 copy-start.18
  1397.8 25.1 copy-start.19
  1397.8 25.1 copy-start.23
  1397.8 25.1 copy-start.24
  1397.8 25.1 copy-start.25
  1397.8 25.1 copy-start.31
  1397.8 25.1 copy-start.32
  1397.8 25.1 copy-start.36
  1397.9 25.1 copy-start.37
  1397.9 25.1 copy-start.42
  1574.6 25.1 copy-start.18
  1574.6 25.1 copy-start.19
  1574.6 25.1 copy-start.23
  1574.6 25.1 copy-start.24
  1751.8 25.2 copy-start.18
  1751.8 25.2 copy-start.19
  1751.8 25.2 copy-start.23
  1751.8 25.2 copy-start.24
  1751.8 25.2 copy-start.25
  1751.8 25.2 copy-start.31
  1751.8 25.2 copy-start.32
  1751.9 25.2 copy-start.36
  1751.9 25.2 copy-start.37
  1751.9 25.2 copy-start.42
  1884.9 25.1 copy-start.18
  1885.0 25.1 copy-start.19
  2124.2 13.3 collective-permute-start.1
  2173.5 493.8 %all-gather.10.cloned.1.call-start = ((), (), s32[]{:S(2)}) async-start(), calls=%async_computation | async-start | bytes 1081344 | tf_op jit(solution)/shard_map/all_gather | solution.py:277
  2611.9 135.7 %all-gather.14.cloned.1.call-start = ((), (), s32[]{:S(2)}) async-start(), calls=%async_computation.2 | async-start | bytes 8650752 | tf_op jit(solution)/shard_map/all_gather | solution.py:276
  2613.6 251.5 %all-gather.12.cloned.1.call-start = ((), (), s32[]{:S(2)}) async-start(), calls=%async_computation.1 | async-start | bytes 17301504 | tf_op jit(solution)/shard_map/all_gather | solution.py:275
  2756.8 126.6 %copy-start.20 = (f32[2048,96]{0,1:T(8,128)S(1)}, f32[2048,96]{0,1:T(8,128)}, u32[]{:S(2)}) copy-start(f32[2048,96]{0,1:T(8,128)} %get-tuple-element.2964) | copy-start | bytes 2359300
  2756.8 127.4 %copy-start.28 = (f32[64,2048]{1,0:T(8,128)S(1)}, f32[64,2048]{1,0:T(8,128)}, u32[]{:S(2)}) copy-start(f32[64,2048]{1,0:T(8,128)} %get-tuple-element.2965) | copy-start | bytes 1572868
  2756.8 128.2 %copy-start.44 = (f32[16,2048]{1,0:T(8,128)S(1)}, f32[16,2048]{1,0:T(8,128)}, u32[]{:S(2)}) copy-start(f32[16,2048]{1,0:T(8,128)} %get-tuple-element.2967) | copy-start | bytes 393220
  (429 other events, 8954.0 us)
Sparse Core Ops, SparseCore 0:
  45.9 24.6 all-gather.15
  224.8 24.6 all-gather.19
  391.4 24.6 all-gather.17
  2173.6 436.7 all-reduce.6
  2614.3 52.9 all-gather.9
  2671.1 76.3 all-gather.13
  2751.6 113.4 all-gather.11
where the time goes:
time: 2950 us; the launch traced here: 2890 us
  other arithmetic  1260 us (43%)
  local copies, waits for them, and re-layouts  777 us (26%)
  waiting for transfers between devices  645 us (22%)
  loops' own time  99.3 us (3%)
  matrix products  49.7 us (2%)
  blocking collectives  40.4 us (1%)
    unnamed x8, waiting for transfers between devices  437 us
    reduce_sum x320, other arithmetic, back_full(): jnp.sum(through * rates, axis=1) + active_now * weighted  373 us
    mul x96, other arithmetic, grow_block(): delta_block[:, place] * active_block[:, place]  218 us
    another operation x128, local copies, waits for them, and re-layouts, back_full(): jnp.stack(pieces[::-1], axis=1)  167 us
    add x96, other arithmetic, back_full(): jnp.sum(through * rates, axis=1) + active_now * weighted  146 us
    reduce_sum x160, other arithmetic, back_full(): weighted = jnp.sum(adjoint * inject_block[:, place, :, None], axis=1)  132 us
    reduce_sum x128, other arithmetic, back_full(): pieces_read.append(jnp.sum(grad_now[:, None, :] * kept[place], axis=2))  119 us
    all_gather x1, waiting for transfers between devices, on_device(): lax.all_gather(shares[0], ('dp', 'seq'), axis=0, tiled=True)  108 us
  transfers between devices with their start and end apart: 9, of which 5 were waited for; matrix products, arithmetic and copies ran while one was open for 12% of the time, Pallas kernels for 0%

commit v1 on v0

v1 whole, which is shorter than its diff:
```python
import functools
import math

import jax
import jax.numpy as jnp
from jax import lax
from jax.experimental import pallas as pl
from jax.experimental.pallas import tpu as pltpu
from jax.sharding import PartitionSpec as P

EPS = 1e-05
LANES = 128
SUB = 8
LOG2E = math.log2(math.e)
LN2 = math.log(2.0)
F32 = jnp.float32
BF16 = jnp.bfloat16


def passed_along(value, axis, by):
    peers = lax.axis_size(axis)
    pairs = [(i, i + by) for i in range(peers) if 0 <= i + by < peers]
    return lax.ppermute(value, axis, pairs)


def silu_slope(value):
    sigma = jax.nn.sigmoid(value)
    return sigma * (1.0 + value * (1.0 - sigma))


def contract_rows(left, right):
    return lax.dot_general(
        left, right, (((0,), (0,)), ((), ())), preferred_element_type=F32
    )


def contract_cols(left, right):
    return lax.dot_general(
        left, right, (((1,), (1,)), ((), ())), preferred_element_type=F32
    )


def to_spans(array):
    rows = array.shape[0]
    return array.reshape(SUB, rows // SUB, -1).swapaxes(0, 1).reshape(rows, -1)


def from_spans(array):
    rows = array.shape[0]
    return array.reshape(rows // SUB, SUB, -1).swapaxes(0, 1).reshape(rows, -1)


def sublane(shape):
    return lax.broadcasted_iota(jnp.int32, shape, len(shape) - 2)


def shift_up(value, by, fill, reverse):
    place = sublane(value.shape)
    if reverse:
        moved = pltpu.roll(value, SUB - by, value.ndim - 2)
        return jnp.where(place < SUB - by, moved, fill)
    moved = pltpu.roll(value, by, value.ndim - 2)
    return jnp.where(place >= by, moved, fill)


def expand_columns(select, first, states):
    width = select.shape[1]
    shape = (width, states * LANES)
    source = lax.broadcasted_iota(jnp.int32, shape, 0)
    target = lax.broadcasted_iota(jnp.int32, shape, 1) // LANES + first
    spread = (source == target).astype(F32).astype(BF16)
    return jnp.dot(select, spread, preferred_element_type=F32)


def scaled_rates(decay_ref, rate_scr, states):
    rates = -jnp.exp(decay_ref[...]) * LOG2E
    for n in range(states):
        rate_scr[n] = jnp.broadcast_to(rates[n : n + 1], (SUB, LANES))


def ends_kernel(
    rank, states, pre_ref, active_ref, grad_ref, select_ref, decay_ref,
    sums_ref, ahead_ref, behind_ref, end_ref, message_ref,
    inject_scr, readout_scr, rate_scr, delta_scr, drive_scr,
):
    rows = pre_ref.shape[0]
    steps = rows // SUB

    @pl.when(pl.program_id(0) == 0)
    def _():
        inject_scr[...] = expand_columns(select_ref[...], rank, states)
        readout_scr[...] = expand_columns(select_ref[...], rank + states, states)

    scaled_rates(decay_ref, rate_scr, states)
    delta = jax.nn.softplus(pre_ref[...])
    delta_scr[...] = delta
    drive_scr[...] = delta * active_ref[...].astype(F32)
    unroll = 2

    def body(i, carry):
        total, state, message, decay = carry
        state, message, decay = list(state), list(message), list(decay)
        for u in range(unroll):
            here = pl.ds(pl.multiple_of((i * unroll + u) * SUB, SUB), SUB)
            d, drive, g = delta_scr[here, :], drive_scr[here, :], grad_ref[here, :]
            total = total + d
            for n in range(states):
                cols = pl.ds(n * LANES, LANES)
                factor = jnp.exp2(d * rate_scr[n])
                state[n] = factor * state[n] + drive * inject_scr[here, cols]
                decay[n] = decay[n] * factor
                message[n] = message[n] + decay[n] * (g * readout_scr[here, cols])
        return total, tuple(state), tuple(message), tuple(decay)

    zero = jnp.zeros((SUB, LANES), F32)
    total, state, message, decay = lax.fori_loop(
        0, steps // unroll, body,
        (zero, (zero,) * states, (zero,) * states, (jnp.ones((SUB, LANES), F32),) * states),
    )
    sums_ref[...] = total
    for n in range(states):
        for value, out, edge, reverse in (
            (state[n], ahead_ref, end_ref, False), (message[n], behind_ref, message_ref, True)
        ):
            factor = decay[n]
            for by in (1, 2, 4):
                value = value + factor * shift_up(value, by, 0.0, reverse)
                factor = factor * shift_up(factor, by, 1.0, reverse)
            out[n] = shift_up(value, 1, 0.0, reverse)
            last = 0 if reverse else SUB - 1
            edge[n : n + 1, :] = value[last : last + 1]


def scan_kernel(
    rank, states, pre_ref, active_ref, gate_ref, graded_ref, select_ref, decay_ref, skip_ref,
    ahead_ref, behind_ref, start_ref, incoming_ref,
    gated_ref, dgate_ref, dprelow_ref, dactive_ref, drate_ref, dbias_ref, dskip_ref, dselect_ref,
    inject_scr, readout_scr, rate_scr, delta_scr, drive_scr, grad_scr, scanned_scr,
    state_scr, factor_scr, dread_scr, dinject_scr,
):
    rows = pre_ref.shape[0]
    steps = rows // SUB

    @pl.when(pl.program_id(0) == 0)
    def _():
        inject_scr[...] = expand_columns(select_ref[...], rank, states)
        readout_scr[...] = expand_columns(select_ref[...], rank + states, states)
        dread_scr[...] = jnp.zeros_like(dread_scr)
        dinject_scr[...] = jnp.zeros_like(dinject_scr)

    scaled_rates(decay_ref, rate_scr, states)
    delta = jax.nn.softplus(pre_ref[...])
    delta_scr[...] = delta
    drive_scr[...] = delta * active_ref[...].astype(F32)
    gate = gate_ref[...].astype(F32)
    grad_scr[...] = graded_ref[...] * (gate * jax.nn.sigmoid(gate))
    total = jnp.zeros((SUB, LANES), F32)
    for j in range(steps):
        total = total + delta_scr[j * SUB : (j + 1) * SUB]
    before, after = total, total
    for by in (1, 2, 4):
        before = before + shift_up(before, by, 0.0, False)
        after = after + shift_up(after, by, 0.0, True)
    before, after = before - total, after - total
    unroll = 2
    begin = []
    for n in range(states):
        reach = jnp.exp2(before * rate_scr[n])
        begin.append(ahead_ref[n] + reach * start_ref[n : n + 1, :])
        state_scr[n] = begin[-1]

    def forward(i, state):
        state = list(state)
        for u in range(unroll):
            j = i * unroll + u
            here = pl.ds(pl.multiple_of(j * SUB, SUB), SUB)
            d, drive, g = delta_scr[here, :], drive_scr[here, :], grad_scr[here, :]
            sums = [None] * 4
            for n in range(states):
                cols = pl.ds(n * LANES, LANES)
                factor = jnp.exp2(d * rate_scr[n])
                factor_scr[j * states + n] = factor
                state[n] = factor * state[n] + drive * inject_scr[here, cols]
                state_scr[(j + 1) * states + n] = state[n]
                dread_scr[here, cols] += g * state[n]
                term = readout_scr[here, cols] * state[n]
                sums[n % 4] = term if sums[n % 4] is None else sums[n % 4] + term
            scanned_scr[here, :] = (sums[0] + sums[1]) + (sums[2] + sums[3])
        return tuple(state)

    lax.fori_loop(0, steps // unroll, forward, tuple(begin))

    active = active_ref[...].astype(F32)
    skip = skip_ref[...]
    gate = gate_ref[...].astype(F32)
    sigma = jax.nn.sigmoid(gate)
    scanned = scanned_scr[...] + skip * active
    gated_ref[...] = (scanned * (gate * sigma)).astype(BF16)
    dgate_ref[...] = (
        graded_ref[...] * scanned * (sigma * (1.0 + gate * (1.0 - sigma)))
    ).astype(BF16)
    dskip_ref[...] = jnp.sum(grad_scr[...] * active, axis=0, keepdims=True)

    adjoint0, zeros = [], (jnp.zeros((SUB, LANES), F32),) * states
    for n in range(states):
        reach = jnp.exp2(after * rate_scr[n])
        adjoint0.append(behind_ref[n] + reach * incoming_ref[n : n + 1, :])

    def backward(i, carry):
        adjoint, total = list(carry[0]), list(carry[1])
        for u in range(unroll):
            j = steps - 1 - (i * unroll + u)
            here = pl.ds(pl.multiple_of(j * SUB, SUB), SUB)
            d, drive, g = delta_scr[here, :], drive_scr[here, :], grad_scr[here, :]
            dsum, weighted = [None] * 4, [None] * 4
            for n in range(states):
                cols = pl.ds(n * LANES, LANES)
                whole = adjoint[n] + g * readout_scr[here, cols]
                adjoint[n] = factor_scr[j * states + n] * whole
                through = adjoint[n] * state_scr[j * states + n]
                total[n] = total[n] + through * d
                dinject_scr[here, cols] += whole * drive
                term = through * rate_scr[n]
                dsum[n % 4] = term if dsum[n % 4] is None else dsum[n % 4] + term
                term = whole * inject_scr[here, cols]
                weighted[n % 4] = term if weighted[n % 4] is None else weighted[n % 4] + term
            weight = (weighted[0] + weighted[1]) + (weighted[2] + weighted[3])
            dsums = (dsum[0] + dsum[1]) + (dsum[2] + dsum[3])
            dactive_ref[here, :] = d * weight
            scanned_scr[here, :] = dsums * LN2
            grad_scr[here, :] = weight
        return tuple(adjoint), tuple(total)

    dskipped = skip * grad_scr[...]
    unused, total = lax.fori_loop(0, steps // unroll, backward, (tuple(adjoint0), zeros))
    dactive_ref[...] = dactive_ref[...] + skip * (graded_ref[...] * (gate * sigma))
    dpre = (scanned_scr[...] + active * grad_scr[...]) * jax.nn.sigmoid(pre_ref[...])
    dprelow_ref[...] = dpre.astype(BF16)
    dbias_ref[...] = jnp.sum(dpre, axis=0, keepdims=True)
    for n in range(states):
        drate_ref[n : n + 1, :] = (
            jnp.sum(total[n], axis=0, keepdims=True) * rate_scr[n, 0:1] * LN2
        )

    @pl.when(pl.program_id(0) == pl.num_programs(0) - 1)
    def _():
        shape = (states * LANES, 2 * states)
        for first, scr in ((0, dinject_scr), (states, dread_scr)):
            gather = (
                lax.broadcasted_iota(jnp.int32, shape, 0) // LANES + first
                == lax.broadcasted_iota(jnp.int32, shape, 1)
            ).astype(F32).astype(BF16)
            high = scr[...].astype(BF16)
            low = (scr[...] - high.astype(F32)).astype(BF16)
            part = jnp.dot(high, gather, preferred_element_type=F32) + jnp.dot(
                low, gather, preferred_element_type=F32
            )
            if first == 0:
                dselect_ref[...] = part
            else:
                dselect_ref[...] += part


def run_ends(pre, active, grad, select, decay_log, rank):
    rows, inner = pre.shape
    states = decay_log.shape[0]
    tall = pl.BlockSpec((rows, LANES), lambda e: (0, e))
    return pl.pallas_call(
        functools.partial(ends_kernel, rank, states),
        grid=(inner // LANES,),
        in_specs=[
            tall, tall, tall,
            pl.BlockSpec(select.shape, lambda e: (0, 0)),
            pl.BlockSpec((states, LANES), lambda e: (0, e)),
        ],
        out_specs=[
            pl.BlockSpec((SUB, LANES), lambda e: (0, e)),
            pl.BlockSpec((states, SUB, LANES), lambda e: (0, 0, e)),
            pl.BlockSpec((states, SUB, LANES), lambda e: (0, 0, e)),
            pl.BlockSpec((states, LANES), lambda e: (0, e)),
            pl.BlockSpec((states, LANES), lambda e: (0, e)),
        ],
        out_shape=[
            jax.ShapeDtypeStruct((SUB, inner), F32),
            jax.ShapeDtypeStruct((states, SUB, inner), F32),
            jax.ShapeDtypeStruct((states, SUB, inner), F32),
            jax.ShapeDtypeStruct((states, inner), F32),
            jax.ShapeDtypeStruct((states, inner), F32),
        ],
        scratch_shapes=[
            pltpu.VMEM((rows, states * LANES), F32),
            pltpu.VMEM((rows, states * LANES), F32),
            pltpu.VMEM((states, SUB, LANES), F32),
            pltpu.VMEM((rows, LANES), F32),
            pltpu.VMEM((rows, LANES), F32),
        ],
        compiler_params=pltpu.CompilerParams(vmem_limit_bytes=48 << 20),
        name="span_ends",
    )(pre, active, grad, select, decay_log)


def run_scan(pre, active, gate, graded, select, decay_log, skip, ahead, behind, start, incoming, rank):
    rows, inner = pre.shape
    states = decay_log.shape[0]
    tall = pl.BlockSpec((rows, LANES), lambda e: (0, e))
    line = pl.BlockSpec((1, LANES), lambda e: (0, e))
    table = pl.BlockSpec((states, LANES), lambda e: (0, e))
    cube = pl.BlockSpec((states, SUB, LANES), lambda e: (0, 0, e))
    wide = pltpu.VMEM((rows, states * LANES), F32)
    thin = pltpu.VMEM((rows, LANES), F32)
    return pl.pallas_call(
        functools.partial(scan_kernel, rank, states),
        grid=(inner // LANES,),
        in_specs=[
            tall, tall, tall, tall,
            pl.BlockSpec(select.shape, lambda e: (0, 0)),
            table, line, cube, cube, table, table,
        ],
        out_specs=[
            tall, tall, tall, tall, table, line, line,
            pl.BlockSpec((rows, 2 * states), lambda e: (0, 0)),
        ],
        out_shape=[
            jax.ShapeDtypeStruct((rows, inner), BF16),
            jax.ShapeDtypeStruct((rows, inner), BF16),
            jax.ShapeDtypeStruct((rows, inner), BF16),
            jax.ShapeDtypeStruct((rows, inner), F32),
            jax.ShapeDtypeStruct((states, inner), F32),
            jax.ShapeDtypeStruct((1, inner), F32),
            jax.ShapeDtypeStruct((1, inner), F32),
            jax.ShapeDtypeStruct((rows, 2 * states), F32),
        ],
        scratch_shapes=[
            wide, wide,
            pltpu.VMEM((states, SUB, LANES), F32),
            thin, thin, thin, thin,
            pltpu.VMEM(((rows // SUB + 1) * states, SUB, LANES), F32),
            pltpu.VMEM((rows // SUB * states, SUB, LANES), F32),
            wide, wide,
        ],
        compiler_params=pltpu.CompilerParams(vmem_limit_bytes=56 << 20),
        name="span_scan",
    )(pre, active, gate, graded, select, decay_log, skip, ahead, behind, start, incoming)


def carried(sums, ends, rates, ahead):
    count = sums.shape[0]
    me = lax.axis_index("seq")
    one = jnp.arange(count)[:, None]
    two = jnp.arange(count)[None, :]
    if ahead:
        between = (two > one) & (two < me)
        used = jnp.arange(count) < me
    else:
        between = (two < one) & (two > me)
        used = jnp.arange(count) > me
    gaps = jnp.sum(jnp.where(between[:, :, None], sums[None], 0.0), axis=1)
    reach = jnp.exp(gaps[:, None, :] * rates[None])
    return jnp.sum(jnp.where(used[:, None, None], reach * ends, 0.0), axis=0)


def on_device(
    byte_ids,
    embedding,
    cotangent,
    norm_gain,
    input_projection_weight,
    conv_weight,
    conv_bias,
    select_weight,
    step_weight,
    step_bias,
    decay_log,
    skip_gain,
    output_projection_weight,
):
    count, stretch = byte_ids.shape
    vocab, width = embedding.shape
    kernel, inner = conv_weight.shape
    states = decay_log.shape[0]
    rank = step_weight.shape[0]
    rows = count * stretch
    halo = kernel - 1
    ids = to_spans(byte_ids.reshape(rows, 1))
    one_hot = ids == jnp.arange(vocab, dtype=jnp.int32)[None, :]
    block_inputs = jnp.dot(one_hot.astype(BF16), embedding, preferred_element_type=F32)
    scale = lax.rsqrt(jnp.mean(block_inputs * block_inputs, axis=1, keepdims=True) + EPS)
    normed_input = (block_inputs * scale * norm_gain).astype(BF16)
    front = jnp.dot(
        normed_input, input_projection_weight[:, :inner], preferred_element_type=F32
    ).astype(BF16)
    gate = jnp.dot(
        normed_input, input_projection_weight[:, inner:], preferred_element_type=F32
    ).astype(BF16)
    last = front[rows - halo * SUB :].reshape(halo, SUB, inner)
    tail = passed_along(last[:, SUB - 1], "seq", 1)
    earlier = jnp.concatenate([tail[:, None], last[:, : SUB - 1]], axis=1)
    extended = jnp.concatenate([earlier.reshape(halo * SUB, inner), front], axis=0).astype(F32)
    mixed = conv_bias + conv_weight[0] * extended[:rows]
    for place in range(1, kernel):
        mixed = mixed + conv_weight[place] * extended[place * SUB : place * SUB + rows]
    active = jax.nn.silu(mixed).astype(BF16)
    select = jnp.dot(active, select_weight, preferred_element_type=F32).astype(BF16)
    lowrank = select[:, :rank]
    pre = jnp.dot(lowrank, step_weight, preferred_element_type=F32) + step_bias
    rates = -jnp.exp(decay_log)
    upstream = to_spans(cotangent.reshape(rows, width))
    graded = contract_cols(upstream, output_projection_weight)
    gate_real = gate.astype(F32)
    grad = graded * jax.nn.silu(gate_real)

    sums, ahead, behind, end, message = run_ends(pre, active, grad, select, decay_log, rank)
    all_sums = lax.all_gather(jnp.sum(sums, axis=0), "seq")
    all_ends = lax.all_gather(jnp.stack([end, message]), "seq")
    start = carried(all_sums, all_ends[:, 0], rates, True)
    incoming = carried(all_sums, all_ends[:, 1], rates, False)
    gated, d_gate, d_pre_low, d_active, d_decay_log, d_step_bias, d_skip_gain, d_pair = run_scan(
        pre, active, gate, graded, select, decay_log, skip_gain.reshape(1, inner),
        ahead, behind, start, incoming, rank,
    )

    result = block_inputs + jnp.dot(gated, output_projection_weight, preferred_element_type=F32)
    output = from_spans(result.astype(BF16)).reshape(count, stretch, width)
    d_output_weight = contract_rows(gated, upstream)
    d_step_weight = contract_rows(lowrank, d_pre_low)
    d_lowrank = contract_cols(d_pre_low, step_weight)
    d_select = jnp.concatenate([d_lowrank, d_pair], axis=1).astype(BF16)
    d_select_weight = contract_rows(active, d_select)
    d_mixed = (d_active + contract_cols(d_select, select_weight)) * silu_slope(mixed)
    d_conv_bias = jnp.sum(d_mixed, axis=0)
    d_conv_weight = jnp.stack(
        [
            jnp.sum(d_mixed * extended[place * SUB : place * SUB + rows], axis=0)
            for place in range(kernel)
        ]
    )
    first = d_mixed[: halo * SUB].reshape(halo, SUB, inner)
    after = passed_along(first[:, 0], "seq", -1)
    later = jnp.concatenate([first[:, 1:], after[:, None]], axis=1)
    spread = jnp.concatenate([d_mixed, later.reshape(halo * SUB, inner)], axis=0)
    d_front = conv_weight[halo] * spread[:rows]
    for place in range(1, kernel):
        d_front = d_front + conv_weight[halo - place] * spread[place * SUB : place * SUB + rows]
    d_both = jnp.concatenate([d_front.astype(BF16), d_gate], axis=1)
    d_input_weight = contract_rows(normed_input, d_both)
    d_normed = contract_cols(d_both, input_projection_weight)
    d_norm_gain = jnp.sum(d_normed * block_inputs * scale, axis=0)
    scaled = norm_gain * d_normed
    cubed = scale * scale * scale
    d_inputs = (
        upstream.astype(F32)
        + scale * scaled
        - block_inputs * cubed * jnp.mean(scaled * block_inputs, axis=1, keepdims=True)
    )
    high = d_inputs.astype(BF16)
    low = (d_inputs - high.astype(F32)).astype(BF16)
    hot = one_hot.astype(BF16)
    d_embedding = contract_rows(hot, high) + contract_rows(hot, low)
    everywhere = ("dp", "seq")
    large = [
        lax.psum(part.astype(BF16), everywhere).astype(F32)
        for part in (d_output_weight, d_input_weight, d_embedding)
    ]
    small = lax.psum(
        (
            d_norm_gain,
            d_conv_weight,
            d_conv_bias,
            d_select_weight,
            d_step_weight,
            d_step_bias.reshape(inner),
            d_decay_log,
            d_skip_gain.reshape(inner),
        ),
        everywhere,
    )
    return (
        output,
        from_spans(d_inputs).reshape(count, stretch, width),
        large[2],
        small[0],
        large[1],
        small[1],
        small[2],
        small[3],
        small[4],
        small[5],
        small[6],
        small[7],
        large[0],
    )


def solution(mesh):
    placed = (P("dp", "seq"), P(), P("dp", "seq", None)) + (P(),) * 10
    return jax.shard_map(
        on_device,
        mesh=mesh,
        in_specs=placed,
        out_specs=(P("dp", "seq", None), P("dp", "seq", None)) + (P(),) * 11,
        check_vma=False,
    )
```

time: 2950 us -> 634 us (0.21); the launches traced: 2890 us -> 625 us
  other arithmetic: 1260 us -> 39.7 us
  local copies, waits for them, and re-layouts: 777 us -> 17.3 us
  waiting for transfers between devices: 645 us -> 317 us
  Pallas kernels: 0 us -> 112 us
  loops' own time: 99.3 us -> 0 us
    reduce_sum x803 -> x4, other arithmetic: 696 us -> 12.7 us  [the longest x1 9.64 us: on_device(): jnp.sum(d_mixed * extended[place * SUB:place * SUB + rows], axis=0)]
    unnamed x8 -> x3, waiting for transfers between devices: 437 us -> 0.05 us
    psum x0 -> x2, waiting for transfers between devices: none -> 301 us  [the longest x1 180 us: on_device(): lax.psum(part.astype(BF16), everywhere).astype(F32)]
    add x199 -> x0, other arithmetic: 283 us -> none  [the longest x96 146 us: back_full(): jnp.sum(through * rates, axis=1) + active_now * weighted]
    mul x545 -> x0, other arithmetic: 264 us -> none  [the longest x96 218 us: grow_block(): delta_block[:, place] * active_block[:, place]]
    mul x192 -> x0, local copies, waits for them, and re-layouts: 207 us -> none  [the longest x96 103 us: grow_block(): (delta_block[:, place] * active_block[:, place])[:, None, :]]
    all_gather x6 -> x1, waiting for transfers between devices: 208 us -> 16.3 us  [on_device(): all_ends = lax.all_gather(jnp.stack([end, message]), 'seq')]
    another operation x170 -> x3, local copies, waits for them, and re-layouts: 185 us -> 0.25 us  [the longest x2 0.17 us: to_spans(): return array.reshape(SUB, rows // SUB, -1).swapaxes(0, 1).reshape(rows, -1)]
  transfers between devices with their start and end apart: 9 -> 5, of which waited for: 5 -> 3; matrix products, arithmetic and copies ran while one was open for 12% -> 7% of each run, Pallas kernels for 0% -> 0%
where the time goes in v1:
time: 634 us; the launch traced here: 625 us
  waiting for transfers between devices  317 us (50%)
  Pallas kernels  112 us (18%)
  matrix products  61.6 us (10%)
  blocking collectives  58.8 us (9%)
  other arithmetic  39.7 us (6%)
  local copies, waits for them, and re-layouts  17.3 us (3%)
  between operations  14.9 us (2%)
    psum x1, waiting for transfers between devices, on_device(): lax.psum(part.astype(BF16), everywhere).astype(F32)  180 us
    psum x1, waiting for transfers between devices, on_device(): lax.psum((d_norm_gain, d_conv_weight, d_conv_bias, d_select_weight, d_ste...  121 us
    pallas_call x1, Pallas kernels, run_scan(): pl.pallas_call(functools.partial(scan_kernel, rank, states), grid=(inner...  77.1 us
    psum x1, blocking collectives, on_device(): lax.psum((d_norm_gain, d_conv_weight, d_conv_bias, d_select_weight, d_ste...  43.4 us
    pallas_call x1, Pallas kernels, run_ends(): pl.pallas_call(functools.partial(ends_kernel, rank, states), grid=(inner...  34.6 us
    dot_general x4, matrix products, contract_cols(): lax.dot_general(left, right, (((1,), (1,)), ((), ())), preferred_element_...  22 us
    dot_general x6, matrix products, contract_rows(): lax.dot_general(left, right, (((0,), (0,)), ((), ())), preferred_element_...  21.4 us
    convert_element_type x3, other arithmetic, on_device(): lax.psum(part.astype(BF16), everywhere).astype(F32)  17.5 us
  transfers between devices with their start and end apart: 5, of which 3 were waited for; matrix products, arithmetic and copies ran while one was open for 7% of the time, Pallas kernels for 0%

profile of v1, /device:TPU:0, one launch (start us, length us, event | category | flops | bytes accessed | tf_op | source)
XLA Modules:
  0.0 625.3 jit_solution(10068829831052078634)
XLA Ops:
  7.8 1.3 reduce.3
  9.4 0.6 multiply_reduce_fusion.6
  9.9 1.3 copy-done.12
  11.3 1.1 multiply_convert_fusion.1
  12.4 5.1 fusion.17
  17.6 2.6 collective-permute-start
  20.2 2.4 fusion.20.gate_ref
  22.6 6.1 fusion.11
  28.9 0.6 maximum_convert_fusion
  29.5 3.7 multiply_convert_fusion
  33.2 0.7 convolution_convert_fusion.2.select_ref
  34.0 2.7 convolution_add_fusion.pre_ref
  36.7 34.6 %span_ends.1 = (f32[8,2048]{1,0:T(8,128)S(1)}, f32[16,8,2048]{2,1,0:T(8,128)S(1)}, f32[16,8,2048]{2,1,0:T(8,128)S(1)}, f32[16,2048]{1,0:T(8,128)S(1)}, f32[16,2048]{1,0:T(8,128)S(1)}) custom-call(f32[512,2048]{1,0:T(8,128)} %convolution_add_fusion.pre_ref, bf16[512,2048]{1,0:T(8,128)(2,1)S(1)} %get-tuple-element.61.active_ref, ...), custom_call_target="tpu_custom_call" | custom-call | tf_op jit(solution)/shard_map/span_ends/pallas_call | solution.py:268
  71.3 1.0 copy-done.7
  72.2 1.0 copy-done.8
  73.2 0.7 pad_maximum_fusion.4
  74.1 15.4 %all-gather = f32[16384]{0:T(1024)S(1)} all-gather(f32[2048]{0:T(1024)S(1)} %reduce_sum.118), channel_id=2, replica_groups=mesh['dp'=4,'seq'=8] {'seq'}, dimensions={0}, use_global_device_ids=true | all-gather | bytes 73728 | tf_op jit(solution)/shard_map/all_gather | solution.py:413
  89.9 16.3 %all-gather.4.cloned.1.call-done = f32[16,16,2048]{2,1,0:T(8,128)} async-done(((f32[2,16,2048]{2,1,0:T(8,128)}), f32[16,16,2048]{2,1,0:T(8,128)}) %all-gather.4.cloned.1.call-update) | async-done | bytes 2097168 | tf_op jit(solution)/shard_map/all_gather | solution.py:414
  106.2 2.7 fusion.28
  108.9 77.1 %span_scan.1 = (bf16[512,2048]{1,0:T(8,128)(2,1)}, bf16[512,2048]{1,0:T(8,128)(2,1)}, bf16[512,2048]{1,0:T(8,128)(2,1)}, f32[512,2048]{1,0:T(8,128)}, f32[16,204...) custom-call(f32[512,2048]{1,0:T(8,128)} %convolution_add_fusion.pre_ref, ...), custom_call_target="tpu_custom_call" | custom-call | tf_op jit(solution)/shard_map/span_scan/pallas_call | solution.py:311
  186.0 1.0 convert.7
  187.0 2.4 convolution_convert_fusion.3
  189.4 5.3 multiply_multiply_fusion
  194.8 1.9 copy-done.14
  196.7 1.3 collective-permute-start.1
  198.0 4.5 convolution_convert_fusion.1
  202.7 9.6 %multiply_reduce_fusion.3 = (f32[2048]{0:T(1024)S(1)}, f32[2048]{0:T(1024)S(1)}, f32[2048]{0:T(1024)S(1)}, f32[2048]{0:T(1024)S(1)}, f32[2048]{0:T(1024)S(1)}, /*index=5*/bf16[512,2048]{1,0:T(8,128)(2,1)}) fusion(f32[512,2048]{1,0:T(8,128)} %copy-done.14, f32[536,2048]{1,0:T(8,128)S(1)} %bitcast.91, f32[24,2048]{1,0:T(8,128)S(1)} %maximum_bitcast_fusion, ...), kind=kLoop, calls=%fused_computation.25 | loop fusion | flops 20961280 | bytes 23339008 | tf_op jit(solution)/shard_map/reduce_sum | solution.py:433
  212.4 10.7 %convolution_convert_fusion = bf16[1024,4096]{1,0:T(8,128)(2,1)} fusion(bf16[512,1024]{1,0:T(8,128)(2,1)} %copy-done.21, bf16[512,2048]{1,0:T(8,128)(2,1)} %get-tuple-element.35, bf16[512,2048]{1,0:T(8,128)(2,1)} %get-tuple-element.63), kind=kOutput, calls=%fused_computation | convolution fusion | flops 4307550208 | bytes 13631488 | tf_op jit(solution)/shard_map/dot_general | solution.py:32
  223.1 8.2 %multiply_reduce_fusion.4 = (f32[1024]{0:T(1024)S(1)}, f32[512]{0:T(512)S(1)}, f32[512,1024]{1,0:T(8,128)S(1)}) fusion(f32[512,1024]{1,0:T(8,128)S(1)} %copy-done.13, f32[512]{0:T(512)S(1)} %get-tuple-element.69, f32[1024]{0:T(1024)S(1)} %copy-done.24, bf16[1024,4096]{1,0:T(8,128)(2,1)} %param.17, bf16[512,2048]{1,0:T(8,128)(2,1)S(1)} %copy-done.31, ...), kind=kOutput, calls=%fused_computation.40 | convolution fusion | flops 4306500096 | bytes 16789504 | tf_op jit(solution)/shard_map/dot_general | solution.py:38
  231.3 1.0 multiply_subtract_fusion
  232.3 0.6 fusion.38
  232.9 0.7 copy-done.10
  233.6 1.4 fusion.25
  235.3 0.6 copy-done.5
  235.9 2.9 fusion.44
  238.8 1.4 fusion.47
  240.2 6.9 %fusion.24 = bf16[8,64,1024]{2,0,1:T(8,128)(2,1)S(1)} fusion(f32[512,1024]{1,0:T(8,128)} %copy-done.12, bf16[512,2048]{1,0:T(8,128)(2,1)} %get-tuple-element.31, bf16[2048,1024]{1,0:T(8,128)(2,1)} %param.25), kind=kOutput, calls=%fused_computation.47 | convolution fusion | flops 2148532224 | bytes 9437184 | tf_op jit(solution)/shard_map/dot_general | solution.py:422
  247.0 1.5 copy.60
  248.6 2.5 copy.63
  251.2 43.4 %all-reduce = (f32[1024]{0:T(1024)}, f32[4,2048]{1,0:T(4,128)}, f32[2048]{0:T(1024)}, f32[2048]{0:T(1024)}, f32[2048]{0:T(1024)}) all-reduce(f32[1024]{0:T(1024)S(1)} %get-tuple-element.44, f32[4,2048]{1,0:T(4,128)S(1)} %pad_maximum_fusion.8, f32[2048]{0:T(1024)S(1)} %get-tuple-element.43, ...), channel_id=1, replica_groups=mesh['dp'=4,'seq'=8] {'dp','seq'}, use_global_device_ids=true, to_apply=%region_9.10 | all-reduce | flops 15360 | bytes 122880 | tf_op jit(solution)/shard_map/psum | solution.py:464
  294.5 179.5 %all-reduce.8.cloned.1.call-done = (bf16[256,1024]{1,0:T(8,128)(2,1)}, bf16[1024,4096]{1,0:T(8,128)(2,1)}, bf16[2048,1024]{1,0:T(8,128)(2,1)}) async-done(((bf16[256,1024]{1,0:T(8,128)(2,1)}, bf16[1024,4096]{1,0:T(8,128)(2,1)}, bf16[2048,1024]{1,0:T(8,128)(2,1)}), (bf16[256,1024]{1,0:T(8,128)(2,1)}, bf16[1024,4096]{1,0:T(8,128)(2,1)}, bf16[2048,1024]{1,0:T(8,128)(2,1)})) %all-reduce.8.cloned.1.call-update) | async-done | bytes 13107216 | tf_op jit(solution)/shard_map/psum | solution.py:461
  474.1 12.0 %convert_element_type.76 = f32[1024,4096]{1,0:T(8,128)} convert(bf16[1024,4096]{1,0:T(8,128)(2,1)} %get-tuple-element.59) | non-fusion elementwise | flops 4194304 | bytes 25165824 | tf_op jit(solution)/shard_map/convert_element_type | solution.py:461
  486.1 4.4 convert_element_type.78
  490.5 1.1 convert_element_type.74
  491.6 121.3 %all-reduce.6.cloned.1.call-done = (f32[2048,96]{0,1:T(8,128)}, f32[64,2048]{1,0:T(8,128)}, f32[16,2048]{1,0:T(8,128)}) async-done(((f32[2048,96]{0,1:T(8,128)}, f32[64,2048]{1,0:T(8,128)}, f32[16,2048]{1,0:T(8,128)}), (f32[2048,96]{0,1:T(8,128)}, f32[64,2048]{1,0:T(8,128)}, f32[16,2048]{1,0:T(8,128)})) %all-reduce.6.cloned.1.call-update) | async-done | bytes 1441808 | tf_op jit(solution)/shard_map/psum | solution.py:464
  612.8 2.1 copy.89
  614.9 1.9 copy.90
  616.8 1.6 copy.91
  (105 shorter events, 2.2 us)
Async XLA Ops:
  7.2 2.2 copy-start
  7.2 99.0 %all-gather.4.cloned.1.call-start = ((), (), s32[]{:S(2)}) async-start(), calls=%async_computation | async-start | bytes 2359296 | tf_op jit(solution)/shard_map/all_gather | solution.py:414
  9.9 1.3 copy-start.12
  11.2 8.9 %slice-start.2 = ((s8[8388608]{0:T(1024)(128)(4,1)}), s8[4194304]{0:T(1024)(128)(4,1)S(1)}, s32[]{:S(2)}) async-start(s8[8388608]{0:T(1024)(128)(4,1)} %bitcast.119), calls=%async_computation.5 | async-start | bytes 8388608
  12.3 7.9 %copy-start.21 = (bf16[512,1024]{1,0:T(8,128)(2,1)}, bf16[512,1024]{1,0:T(8,128)(2,1)S(1)}, u32[]{:S(2)}) copy-start(bf16[512,1024]{1,0:T(8,128)(2,1)S(1)} %multiply_convert_fusion.1) | copy-start | bytes 3145732
  12.3 7.9 %slice-start.3 = ((s8[8388608]{0:T(1024)(128)(4,1)}), s8[4194304]{0:T(1024)(128)(4,1)S(1)}, s32[]{:S(2)}) async-start(s8[8388608]{0:T(1024)(128)(4,1)} %bitcast.119), calls=%async_computation.6 | async-start | bytes 8388608
  17.5 5.1 copy-start.18
  17.5 5.1 copy-start.29
  17.6 11.2 %collective-permute-start = (bf16[3,2048]{1,0:T(4,128)(2,1)S(1)}, bf16[3,2048]{1,0:T(4,128)(2,1)S(1)}, u32[]{:S(2)}, u32[]{:S(2)}) collective-permute-start(bf16[3,2048]{1,0:T(4,128)(2,1)S(1)} %bitcast.114), channel_id=1, source_target_pairs={{0,1},{1,2},{2,3},{3,4},{4,5},{5,6},{6,7},{8,9},{9,10},{10,11},{11... | collective-permute-start | bytes 36872 | tf_op jit(solution)/shard_map/ppermute | solution.py:23
  22.6 6.2 copy-start.16
  22.6 6.1 copy-start.23
  28.8 0.7 copy-start.25
  29.5 3.8 copy-start.9
  29.5 3.8 copy-start.32
  29.5 4.5 copy-start.20
  29.5 4.5 copy-start.26
  33.2 38.0 %copy-start.2 = (bf16[512,2048]{1,0:T(8,128)(2,1)}, bf16[512,2048]{1,0:T(8,128)(2,1)S(1)}, u32[]{:S(2)}) copy-start(bf16[512,2048]{1,0:T(8,128)(2,1)S(1)} %get-tuple-element.61.active_ref) | copy-start | bytes 6291460
  33.2 3.4 copy-start.6
  34.0 37.3 %copy-start.4 = (bf16[512,96]{1,0:T(8,128)(2,1)}, bf16[512,96]{1,0:T(8,128)(2,1)S(1)}, u32[]{:S(2)}) copy-start(bf16[512,96]{1,0:T(8,128)(2,1)S(1)} %convolution_convert_fusion.2.select_ref) | copy-start | bytes 294916
  71.3 1.0 copy-start.7
  72.2 1.0 copy-start.8
  74.0 400.1 %all-reduce.8.cloned.1.call-start = ((), (), s32[]{:S(2)}) async-start(), calls=%async_computation.2 | async-start | bytes 26214400 | tf_op jit(solution)/shard_map/psum | solution.py:461
  189.4 8.6 %copy-start.19 = (bf16[1,512,1024]{2,1,0:T(8,128)(2,1)S(1)}, bf16[1,512,1024]{2,1,0:T(8,128)(2,1)}, u32[]{:S(2)}) copy-start(bf16[1,512,1024]{2,1,0:T(8,128)(2,1)} %param.15) | copy-start | bytes 3145732
  189.4 8.6 %copy-start.30 = (bf16[512,2048]{1,0:T(8,128)(2,1)S(1)}, bf16[512,2048]{1,0:T(8,128)(2,1)}, u32[]{:S(2)}) copy-start(bf16[512,2048]{1,0:T(8,128)(2,1)} %get-tuple-element.31) | copy-start | bytes 6291460
  194.7 2.0 copy-start.14
  196.7 5.9 collective-permute-start.1
  198.0 4.7 slice-start
  198.0 4.7 slice-start.1
  212.3 10.7 %copy-start.13 = (f32[512,1024]{1,0:T(8,128)S(1)}, f32[512,1024]{1,0:T(8,128)}, u32[]{:S(2)}) copy-start(f32[512,1024]{1,0:T(8,128)} %copy-done.12) | copy-start | bytes 6291460
  212.4 10.7 %copy-start.17 = (bf16[512,2048]{1,0:T(8,128)(2,1)S(1)}, bf16[512,2048]{1,0:T(8,128)(2,1)}, u32[]{:S(2)}) copy-start(bf16[512,2048]{1,0:T(8,128)(2,1)} %get-tuple-element.63) | copy-start | bytes 6291460
  212.4 10.7 %copy-start.24 = (f32[1024]{0:T(1024)S(1)}, f32[1024]{0:T(1024)}, u32[]{:S(2)}) copy-start(f32[1024]{0:T(1024)} %param.16) | copy-start | bytes 12292
  212.4 10.7 %copy-start.31 = (bf16[512,2048]{1,0:T(8,128)(2,1)S(1)}, bf16[512,2048]{1,0:T(8,128)(2,1)}, u32[]{:S(2)}) copy-start(bf16[512,2048]{1,0:T(8,128)(2,1)} %get-tuple-element.35) | copy-start | bytes 6291460
  232.3 1.3 copy-start.10
  235.0 0.9 copy-start.5
  235.0 3.8 copy-start.3
  235.0 377.8 %all-reduce.6.cloned.1.call-start = ((), (), s32[]{:S(2)}) async-start(), calls=%async_computation.1 | async-start | bytes 2883584 | tf_op jit(solution)/shard_map/psum | solution.py:464
  240.1 8.4 %copy-start.11 = (f32[512,1024]{1,0:T(8,128)S(1)}, f32[512,1024]{1,0:T(8,128)}, u32[]{:S(2)}) copy-start(f32[512,1024]{1,0:T(8,128)} %copy-done.10) | copy-start | bytes 6291460
  247.0 4.2 copy-start.27
  247.0 4.2 copy-start.28
  474.1 12.0 %copy-start.15 = (bf16[2048,1024]{1,0:T(8,128)(2,1)S(1)}, bf16[2048,1024]{1,0:T(8,128)(2,1)}, u32[]{:S(2)}) copy-start(bf16[2048,1024]{1,0:T(8,128)(2,1)} %get-tuple-element.60) | copy-start | bytes 12582916
  486.1 4.4 copy-start.22
  486.1 132.3 %copy-start.1 = (bf16[256,1024]{1,0:T(8,128)(2,1)S(1)}, bf16[256,1024]{1,0:T(8,128)(2,1)}, u32[]{:S(2)}) copy-start(bf16[256,1024]{1,0:T(8,128)(2,1)} %param.14) | copy-start | bytes 1572868
Sparse Core Ops, SparseCore 0:
  74.1 32.0 all-gather.3
  235.1 238.9 all-reduce.7
  480.3 132.5 all-reduce.5
